TPU v7x, 32 devices: a whole 2x2x4 slice. The times are simulated.
32 devices in a mesh: rep: 8 (over y, x, core), hid: 4 (over z).
Axes of the slice: x: 2, y: 2, z: 4, core: 2. Of those that a mesh axis runs over, the one named last changes fastest.
Arguments:
- tokens: bfloat16 [2, 1024, 1152], P(None, ('rep', 'hid')), may hold values from -6 to 6
- targets: bfloat16 [2, 1024, 1152], P(None, ('rep', 'hid')), may hold values from -6 to 6
- w_gate: float32 [8, 6912, 1152], P('rep', 'hid'), may hold values from -6 to 6
- w_up: float32 [8, 6912, 1152], P('rep', 'hid'), may hold values from -6 to 6
- w_down: float32 [8, 6912, 1152], P('rep', 'hid'), may hold values from -6 to 6
Outputs:
- new_gate: float32 [8, 6912, 1152], P('rep', 'hid')
- new_up: float32 [8, 6912, 1152], P('rep', 'hid')
- new_down: float32 [8, 6912, 1152], P('rep', 'hid')
All inputs are finite; a program needn't handle non-finite values.
Results may differ from a plain program's by a relative error of at most 0.0086.
Values may be sent and summed in bfloat16 or wider, within the bound.
A program may use at most 128 MiB of HBM per device.

v0:
```python
import jax
import jax.numpy as jnp
from jax import lax
from jax.sharding import PartitionSpec as P

D = 1152
FF = 6912
STEPS = 2


LEARNING_RATE = 0.5


def swapped(value, axis, distance):
    mask = 2**distance
    pairs = [(source, source ^ mask) for source in range(lax.axis_size(axis))]
    return lax.ppermute(value, axis, pairs)


def gelu_tanh(value):
    return jax.nn.gelu(value, approximate=True)


def contract_cols(left, right):
    return lax.dot_general(
        left, right, (((1,), (1,)), ((), ())), preferred_element_type=jnp.float32
    )


def contract_rows(left, right):
    return lax.dot_general(
        left, right, (((0,), (0,)), ((), ())), preferred_element_type=jnp.float32
    )


def local(tokens, targets, w_gate, w_up, w_down):
    scale_model = float(D) ** (-0.5)
    scale_hidden = float(FF) ** (-0.5)
    all_tokens, all_targets = (
        lax.all_gather(tokens, "hid", axis=1, tiled=True),
        lax.all_gather(targets, "hid", axis=1, tiled=True),
    )
    weights = (w_gate[0], w_up[0], w_down[0])
    for step_index in range(STEPS):
        token_batch = all_tokens[step_index]
        partner_old = swapped(weights, "rep", step_index)
        gate_half = weights[0].astype(jnp.bfloat16)
        up_half = weights[1].astype(jnp.bfloat16)
        down_half = weights[2].astype(jnp.bfloat16)
        gate_value = contract_cols(token_batch, gate_half) * scale_model
        up_value = contract_cols(token_batch, up_half) * scale_model
        activated, gelu_back = jax.vjp(gelu_tanh, gate_value)
        hidden = (activated * up_value).astype(jnp.bfloat16)
        partial_out = jnp.dot(hidden, down_half, preferred_element_type=jnp.float32) * scale_hidden
        output = lax.psum(partial_out, "hid")
        residual = (output - all_targets[step_index].astype(jnp.float32)).astype(jnp.bfloat16)
        grad_down = contract_rows(hidden, residual) * scale_hidden
        hidden_grad = contract_cols(residual, down_half) * scale_hidden
        gate_grad = gelu_back(hidden_grad * up_value)[0].astype(jnp.bfloat16)
        up_grad = (hidden_grad * activated).astype(jnp.bfloat16)
        grad_gate = contract_rows(gate_grad, token_batch) * scale_model
        grad_up = contract_rows(up_grad, token_batch) * scale_model
        gradients = (grad_gate, grad_up, grad_down)
        other_tokens, other_gate, other_up, other_hidden, other_residual = swapped(
            (token_batch, gate_grad, up_grad, hidden, residual), "rep", step_index
        )
        partner_grads = (
            contract_rows(other_gate, other_tokens) * scale_model,
            contract_rows(other_up, other_tokens) * scale_model,
            contract_rows(other_hidden, other_residual) * scale_hidden,
        )
        weights = tuple(
            (
                (mine + theirs) * 0.5 - LEARNING_RATE * (own_grad + other_grad) * 0.5
                for mine, theirs, own_grad, other_grad in zip(
                    weights, partner_old, gradients, partner_grads
                )
            )
        )
    return (weights[0][None], weights[1][None], weights[2][None])


def solution(mesh):
    placed = (
        P(None, ("rep", "hid"), None),
        P(None, ("rep", "hid"), None),
        P("rep", "hid", None),
        P("rep", "hid", None),
        P("rep", "hid", None),
    )
    return jax.shard_map(
        local,
        mesh=mesh,
        in_specs=placed,
        out_specs=(P("rep", "hid", None), P("rep", "hid", None), P("rep", "hid", None)),
        check_vma=False,
    )
```

profile of v0, /device:TPU:0, one launch (start us, length us, event | category | flops | bytes accessed | tf_op | source)
XLA Modules:
  0.0 698.9 jit_solution(4539646955181789548)
XLA Ops:
  8.3 19.0 %all_gather.6 = bf16[2,128,1152]{2,1,0:T(8,128)(2,1)S(1)} all-gather(bf16[2,32,1152]{2,1,0:T(8,128)(2,1)} %param.5), channel_id=1, replica_groups=mesh['rep'=8,'hid'=4] {'hid'}, dimensions={1}, use_global_device_ids=true | all-gather | bytes 737280 | tf_op jit(solution)/shard_map/all_gather | solution.py:40
  27.2 4.7 fusion.22
  34.2 2.7 convolution_multiply_fusion.1
  37.8 23.6 %all_gather.7 = bf16[2,128,1152]{2,1,0:T(8,128)(2,1)S(1)} all-gather(bf16[2,32,1152]{2,1,0:T(8,128)(2,1)S(1)} %copy-done.9), channel_id=1, replica_groups=mesh['rep'=8,'hid'=4] {'hid'}, dimensions={1}, use_global_device_ids=true | all-gather | bytes 737280 | tf_op jit(solution)/shard_map/all_gather | solution.py:41
  61.3 21.6 %all-reduce.3.cloned.1.call-done = f32[128,1152]{1,0:T(8,128)} async-done(((f32[128,1152]{1,0:T(8,128)}), f32[128,1152]{1,0:T(8,128)}) %all-reduce.3.cloned.1.call-update) | async-done | bytes 589840 | tf_op jit(solution)/shard_map/psum | solution.py:55
  84.0 5.9 multiply_convert_fusion.2
  89.9 4.4 fusion.56
  94.4 2.3 fusion.66
  96.6 2.3 fusion.57
  100.4 13.0 %multiply_subtract_fusion.1 = f32[1728,1152]{1,0:T(8,128)} fusion(f32[1728,1152]{1,0:T(8,128)} %collective-permute-done.4, f32[1728,1152]{1,0:T(8,128)} %fusion.56, bf16[128,1728]{0,1:T(8,128)(2,1)} %copy-done.8, bf16[128,1152]{1,0:T(8,128)(2,1)} %collective-permute-done.2, f32[1,1728,1152]{2,1,0:T(8,128)} %param.8), kind=kOutput, calls=%fused_computation.16 | convolution fusion | flops 519561216 | bytes 32587776 | tf_op jit(solution)/shard_map/dot_general | solution.py:31
  114.9 11.1 %multiply_subtract_fusion.2 = f32[1728,1152]{1,0:T(8,128)} fusion(f32[1728,1152]{1,0:T(8,128)} %collective-permute-done, f32[1728,1152]{1,0:T(8,128)S(1)} %fusion.57, bf16[128,1728]{0,1:T(8,128)(2,1)} %collective-permute-done.1, bf16[128,1152]{1,0:T(8,128)(2,1)} %collective-permute-done.2, f32[1,1728,1152]{2,1,0:T(8,128)} %param.7), kind=kOutput, calls=%fused_computation.17 | convolution fusion | flops 519561216 | bytes 32587776 | tf_op jit(solution)/shard_map/dot_general | solution.py:31
  126.6 8.9 %multiply_subtract_fusion = f32[1728,1152]{1,0:T(8,128)} fusion(f32[1728,1152]{1,0:T(8,128)} %collective-permute-done.6, f32[1728,1152]{1,0:T(8,128)S(1)} %fusion.66, bf16[128,1728]{0,1:T(8,128)(2,1)} %collective-permute-done.7, bf16[128,1152]{1,0:T(8,128)(2,1)} %collective-permute-done.8, f32[1,1728,1152]{2,1,0:T(8,128)S(1)} %bitcast.108), kind=kOutput, calls=%fused_computation.15 | convolution fusion | flops 519561216 | bytes 32587776 | tf_op jit(solution)/shard_map/dot_general | solution.py:31
  136.9 4.5 fusion.31
  141.4 5.7 multiply_convert_fusion.1
  147.2 5.0 convolution_multiply_fusion
  152.9 37.4 %all-reduce.5.cloned.1.call-done = f32[128,1152]{1,0:T(8,128)} async-done(((f32[128,1152]{1,0:T(8,128)}), f32[128,1152]{1,0:T(8,128)}) %all-reduce.5.cloned.1.call-update) | async-done | bytes 589840 | tf_op jit(solution)/shard_map/psum | solution.py:55
  191.4 5.8 multiply_convert_fusion
  202.1 2.2 fusion.59
  204.3 431.2 %collective-permute-done.10 = bf16[128,1152]{1,0:T(8,128)(2,1)} collective-permute-done((bf16[128,1152]{1,0:T(8,128)(2,1)}, bf16[128,1152]{1,0:T(8,128)(2,1)}, u32[]{:S(2)}, u32[]{:S(2)}) %collective-permute-start.10) | collective-permute-done | bytes 294944 | tf_op jit(solution)/shard_map/ppermute | solution.py:17
  636.9 7.9 %collective-permute-done.12 = bf16[128,1728]{0,1:T(8,128)(2,1)S(1)} collective-permute-done((bf16[128,1728]{0,1:T(8,128)(2,1)S(1)}, bf16[128,1728]{0,1:T(8,128)(2,1)S(1)}, u32[]{:S(2)}, u32[]{:S(2)}) %collective-permute-start.12) | collective-permute-done | bytes 442400 | tf_op jit(solution)/shard_map/ppermute | solution.py:17
  647.1 11.1 %subtract_bitcast_fusion.1 = f32[1,1728,1152]{2,1,0:T(8,128)} fusion(f32[1728,1152]{1,0:T(8,128)} %multiply_subtract_fusion.1, f32[1728,1152]{1,0:T(8,128)} %collective-permute-done.11, f32[1728,1152]{1,0:T(8,128)S(1)} %fusion.58, bf16[128,1728]{0,1:T(8,128)(2,1)} %copy-done.7, bf16[128,1152]{1,0:T(8,128)(2,1)} %collective-permute-done.10), kind=kOutput, calls=%fused_computation.13 | convolution fusion | flops 519561216 | bytes 32587776 | tf_op jit(solution)/shard_map/dot_general | solution.py:31
  658.2 11.6 %collective-permute-done.9 = bf16[128,1728]{0,1:T(8,128)(2,1)} collective-permute-done((bf16[128,1728]{0,1:T(8,128)(2,1)}, bf16[128,1728]{0,1:T(8,128)(2,1)}, u32[]{:S(2)}, u32[]{:S(2)}) %collective-permute-start.9) | collective-permute-done | bytes 442400 | tf_op jit(solution)/shard_map/ppermute | solution.py:17
  669.8 11.1 %subtract_bitcast_fusion.2 = f32[1,1728,1152]{2,1,0:T(8,128)} fusion(f32[1728,1152]{1,0:T(8,128)} %multiply_subtract_fusion.2, f32[1728,1152]{1,0:T(8,128)} %collective-permute-done.3, f32[1728,1152]{1,0:T(8,128)S(1)} %fusion.59, bf16[128,1728]{0,1:T(8,128)(2,1)} %collective-permute-done.9, bf16[128,1152]{1,0:T(8,128)(2,1)} %collective-permute-done.10), kind=kOutput, calls=%fused_computation.14 | convolution fusion | flops 519561216 | bytes 32587776 | tf_op jit(solution)/shard_map/dot_general | solution.py:31
  680.9 11.1 %subtract_bitcast_fusion = f32[1,1728,1152]{2,1,0:T(8,128)} fusion(f32[1728,1152]{1,0:T(8,128)} %multiply_subtract_fusion, f32[1728,1152]{1,0:T(8,128)} %collective-permute-done.13, f32[1728,1152]{1,0:T(8,128)S(1)} %fusion.67, bf16[128,1728]{0,1:T(8,128)(2,1)} %collective-permute-done.14, bf16[128,1152]{1,0:T(8,128)(2,1)} %collective-permute-done.15), kind=kOutput, calls=%fused_computation.12 | convolution fusion | flops 519561216 | bytes 32587776 | tf_op jit(solution)/shard_map/dot_general | solution.py:31
  (69 shorter events, 20.5 us)
Async XLA Ops:
  7.2 75.7 %all-reduce.3.cloned.1.call-start = ((), (), s32[]{:S(2)}) async-start(), calls=%async_computation | async-start | bytes 1179648 | tf_op jit(solution)/shard_map/psum | solution.py:55
  7.2 24.8 %copy-start = (f32[1,1728,1152]{2,1,0:T(8,128)S(1)}, f32[1,1728,1152]{2,1,0:T(8,128)}, u32[]{:S(2)}) copy-start(f32[1,1728,1152]{2,1,0:T(8,128)} %param.8) | copy-start | bytes 23887876
  7.2 93.1 %collective-permute-start.4 = (f32[1728,1152]{1,0:T(8,128)}, f32[1728,1152]{1,0:T(8,128)}, u32[]{:S(2)}, u32[]{:S(2)}) collective-permute-start(f32[1728,1152]{1,0:T(8,128)} %bitcast.109), channel_id=1, source_target_pairs={{0,4},{4,0},{8,12},{12,8},{16,20},{20,16},{24,28},{28,24},{1,5},{5... | collective-permute-start | bytes 23887880 | tf_op jit(solution)/shard_map/ppermute | solution.py:17
  7.7 107.1 %collective-permute-start = (f32[1728,1152]{1,0:T(8,128)}, f32[1728,1152]{1,0:T(8,128)}, u32[]{:S(2)}, u32[]{:S(2)}) collective-permute-start(f32[1728,1152]{1,0:T(8,128)} %bitcast.110), channel_id=1, source_target_pairs={{0,4},{4,0},{8,12},{12,8},{16,20},{20,16},{24,28},{28,24},{1,5},{5... | collective-permute-start | bytes 23887880 | tf_op jit(solution)/shard_map/ppermute | solution.py:17
  7.8 118.7 %collective-permute-start.6 = (f32[1728,1152]{1,0:T(8,128)}, f32[1728,1152]{1,0:T(8,128)}, u32[]{:S(2)}, u32[]{:S(2)}) collective-permute-start(f32[1728,1152]{1,0:T(8,128)} %bitcast.104), channel_id=1, source_target_pairs={{0,4},{4,0},{8,12},{12,8},{16,20},{20,16},{24,28},{28,24},{1,5},{5... | collective-permute-start | bytes 23887880 | tf_op jit(solution)/shard_map/ppermute | solution.py:17
  27.2 62.7 %copy-start.1 = (bf16[2,128,1152]{2,1,0:T(8,128)(2,1)}, bf16[2,128,1152]{2,1,0:T(8,128)(2,1)S(1)}, u32[]{:S(2)}) copy-start(bf16[2,128,1152]{2,1,0:T(8,128)(2,1)S(1)} %all_gather.6) | copy-start | bytes 1769476
  36.9 153.4 %all-reduce.5.cloned.1.call-start = ((), (), s32[]{:S(2)}) async-start(), calls=%async_computation.1 | async-start | bytes 1179648 | tf_op jit(solution)/shard_map/psum | solution.py:55
  37.8 61.2 %collective-permute-start.2 = (bf16[128,1152]{1,0:T(8,128)(2,1)}, bf16[128,1152]{1,0:T(8,128)(2,1)}, u32[]{:S(2)}, u32[]{:S(2)}) collective-permute-start(bf16[128,1152]{1,0:T(8,128)(2,1)} %get-tuple-element.8), channel_id=1, source_target_pairs={{0,4},{4,0},{8,12},{12,8},{16,20},{20,16},{24,28},{28,24},{1,5},{5... | collective-permute-start | bytes 884744 | tf_op jit(solution)/shard_map/ppermute | solution.py:17
  61.3 33.0 %copy-start.5 = (bf16[2,128,1152]{2,1,0:T(8,128)(2,1)}, bf16[2,128,1152]{2,1,0:T(8,128)(2,1)S(1)}, u32[]{:S(2)}) copy-start(bf16[2,128,1152]{2,1,0:T(8,128)(2,1)S(1)} %all_gather.7) | copy-start | bytes 1769476
  89.9 9.7 %collective-permute-start.5 = (bf16[128,1728]{0,1:T(8,128)(2,1)S(1)}, bf16[128,1728]{0,1:T(8,128)(2,1)S(1)}, u32[]{:S(2)}, u32[]{:S(2)}) collective-permute-start(bf16[128,1728]{0,1:T(8,128)(2,1)S(1)} %get-tuple-element.5), channel_id=1, source_target_pairs={{0,4},{4,0},{8,12},{12,8},{16,20},{20,16},{24,28},{28,24},{1,5},{5... | collective-permute-start | bytes 1327112 | tf_op jit(solution)/shard_map/ppermute | solution.py:17
  96.6 29.9 %slice-start.2 = ((s8[7962624]{0:T(1024)(128)(4,1)}), s8[4194304]{0:T(1024)(128)(4,1)S(1)}, s32[]{:S(2)}) async-start(s8[7962624]{0:T(1024)(128)(4,1)} %bitcast.107), calls=%async_computation.4 | async-start | bytes 8388608
  99.0 27.6 %slice-start.3 = ((s8[7962624]{0:T(1024)(128)(4,1)}), s8[3768320]{0:T(1024)(128)(4,1)S(1)}, s32[]{:S(2)}) async-start(s8[7962624]{0:T(1024)(128)(4,1)} %bitcast.107), calls=%async_computation.5 | async-start | bytes 7536640
  99.0 27.5 %collective-permute-start.7 = (bf16[128,1728]{0,1:T(8,128)(2,1)}, bf16[128,1728]{0,1:T(8,128)(2,1)}, u32[]{:S(2)}, u32[]{:S(2)}) collective-permute-start(bf16[128,1728]{0,1:T(8,128)(2,1)} %get-tuple-element.9), channel_id=1, source_target_pairs={{0,4},{4,0},{8,12},{12,8},{16,20},{20,16},{24,28},{28,24},{1,5},{5... | collective-permute-start | bytes 1327112 | tf_op jit(solution)/shard_map/ppermute | solution.py:17
  99.6 13.8 %collective-permute-start.1 = (bf16[128,1728]{0,1:T(8,128)(2,1)}, bf16[128,1728]{0,1:T(8,128)(2,1)}, u32[]{:S(2)}, u32[]{:S(2)}) collective-permute-start(bf16[128,1728]{0,1:T(8,128)(2,1)} %get-tuple-element.6), channel_id=1, source_target_pairs={{0,4},{4,0},{8,12},{12,8},{16,20},{20,16},{24,28},{28,24},{1,5},{5... | collective-permute-start | bytes 1327112 | tf_op jit(solution)/shard_map/ppermute | solution.py:17
  100.4 26.2 %collective-permute-start.8 = (bf16[128,1152]{1,0:T(8,128)(2,1)S(1)}, bf16[128,1152]{1,0:T(8,128)(2,1)}, u32[]{:S(2)}, u32[]{:S(2)}) collective-permute-start(bf16[128,1152]{1,0:T(8,128)(2,1)S(1)} %fusion.53), channel_id=1, source_target_pairs={{0,4},{4,0},{8,12},{12,8},{16,20},{20,16},{24,28},{28,24},{1,5},{5... | collective-permute-start | bytes 884744 | tf_op jit(solution)/shard_map/ppermute | solution.py:17
  113.4 532.9 %collective-permute-start.11 = (f32[1728,1152]{1,0:T(8,128)}, f32[1728,1152]{1,0:T(8,128)}, u32[]{:S(2)}, u32[]{:S(2)}) collective-permute-start(f32[1728,1152]{1,0:T(8,128)} %multiply_subtract_fusion.1), channel_id=1, source_target_pairs={{0,8},{4,12},{8,0},{12,4},{16,24},{20,28},{24,16},{28,20},{1,9},{5... | collective-permute-start | bytes 23887880 | tf_op jit(solution)/shard_map/ppermute | solution.py:17
  126.0 543.8 %collective-permute-start.3 = (f32[1728,1152]{1,0:T(8,128)}, f32[1728,1152]{1,0:T(8,128)}, u32[]{:S(2)}, u32[]{:S(2)}) collective-permute-start(f32[1728,1152]{1,0:T(8,128)} %multiply_subtract_fusion.2), channel_id=1, source_target_pairs={{0,8},{4,12},{8,0},{12,4},{16,24},{20,28},{24,16},{28,20},{1,9},{5... | collective-permute-start | bytes 23887880 | tf_op jit(solution)/shard_map/ppermute | solution.py:17
  135.5 545.5 %collective-permute-start.13 = (f32[1728,1152]{1,0:T(8,128)}, f32[1728,1152]{1,0:T(8,128)}, u32[]{:S(2)}, u32[]{:S(2)}) collective-permute-start(f32[1728,1152]{1,0:T(8,128)} %multiply_subtract_fusion), channel_id=1, source_target_pairs={{0,8},{4,12},{8,0},{12,4},{16,24},{20,28},{24,16},{28,20},{1,9},{5... | collective-permute-start | bytes 23887880 | tf_op jit(solution)/shard_map/ppermute | solution.py:17
  141.4 48.8 %copy-start.6 = (bf16[2,128,1152]{2,1,0:T(8,128)(2,1)S(1)}, bf16[2,128,1152]{2,1,0:T(8,128)(2,1)}, u32[]{:S(2)}) copy-start(bf16[2,128,1152]{2,1,0:T(8,128)(2,1)} %copy-done.5) | copy-start | bytes 1769476
  152.2 483.2 %collective-permute-start.10 = (bf16[128,1152]{1,0:T(8,128)(2,1)}, bf16[128,1152]{1,0:T(8,128)(2,1)}, u32[]{:S(2)}, u32[]{:S(2)}) collective-permute-start(bf16[128,1152]{1,0:T(8,128)(2,1)} %get-tuple-element.7), channel_id=1, source_target_pairs={{0,8},{4,12},{8,0},{12,4},{16,24},{20,28},{24,16},{28,20},{1,9},{5... | collective-permute-start | bytes 884744 | tf_op jit(solution)/shard_map/ppermute | solution.py:17
  197.2 447.6 %collective-permute-start.12 = (bf16[128,1728]{0,1:T(8,128)(2,1)S(1)}, bf16[128,1728]{0,1:T(8,128)(2,1)S(1)}, u32[]{:S(2)}, u32[]{:S(2)}) collective-permute-start(bf16[128,1728]{0,1:T(8,128)(2,1)S(1)} %get-tuple-element.3), channel_id=1, source_target_pairs={{0,8},{4,12},{8,0},{12,4},{16,24},{20,28},{24,16},{28,20},{1,9},{5... | collective-permute-start | bytes 1327112 | tf_op jit(solution)/shard_map/ppermute | solution.py:17
  635.4 45.5 %collective-permute-start.14 = (bf16[128,1728]{0,1:T(8,128)(2,1)}, bf16[128,1728]{0,1:T(8,128)(2,1)}, u32[]{:S(2)}, u32[]{:S(2)}) collective-permute-start(bf16[128,1728]{0,1:T(8,128)(2,1)} %get-tuple-element.11), channel_id=1, source_target_pairs={{0,8},{4,12},{8,0},{12,4},{16,24},{20,28},{24,16},{28,20},{1,9},{5... | collective-permute-start | bytes 1327112 | tf_op jit(solution)/shard_map/ppermute | solution.py:17
  644.8 36.1 %collective-permute-start.15 = (bf16[128,1152]{1,0:T(8,128)(2,1)S(1)}, bf16[128,1152]{1,0:T(8,128)(2,1)}, u32[]{:S(2)}, u32[]{:S(2)}) collective-permute-start(bf16[128,1152]{1,0:T(8,128)(2,1)S(1)} %fusion.52), channel_id=1, source_target_pairs={{0,8},{4,12},{8,0},{12,4},{16,24},{20,28},{24,16},{28,20},{1,9},{5... | collective-permute-start | bytes 884744 | tf_op jit(solution)/shard_map/ppermute | solution.py:17
  646.3 23.5 %collective-permute-start.9 = (bf16[128,1728]{0,1:T(8,128)(2,1)}, bf16[128,1728]{0,1:T(8,128)(2,1)}, u32[]{:S(2)}, u32[]{:S(2)}) collective-permute-start(bf16[128,1728]{0,1:T(8,128)(2,1)} %get-tuple-element.4), channel_id=1, source_target_pairs={{0,8},{4,12},{8,0},{12,4},{16,24},{20,28},{24,16},{28,20},{1,9},{5... | collective-permute-start | bytes 1327112 | tf_op jit(solution)/shard_map/ppermute | solution.py:17
  (8 other events, 31.9 us)
Sparse Core Ops, SparseCore 0:
  37.0 45.8 all-reduce.2
  152.4 37.8 all-reduce.4
where the time goes:
time: 699 us
  waiting for transfers between devices  510 us (73%)
  matrix products  117 us (17%)
  blocking collectives  42.5 us (6%)
  between operations  14.2 us (2%)
  starting transfers between devices  11.1 us (2%)
    ppermute x16, waiting for transfers between devices, swapped(): return lax.ppermute(value, axis, pairs)  451 us
    dot_general x12, matrix products, contract_rows(): lax.dot_general(left, right, (((0,), (0,)), ((), ())), preferred_element_...  80.9 us
    psum x2, waiting for transfers between devices, local(): output = lax.psum(partial_out, 'hid')  59 us
    dot_general x6, matrix products, contract_cols(): lax.dot_general(left, right, (((1,), (1,)), ((), ())), preferred_element_...  28.9 us
    all_gather x1, blocking collectives, local(): lax.all_gather(targets, 'hid', axis=1, tiled=True)  23.6 us
    all_gather x1, blocking collectives, local(): lax.all_gather(tokens, 'hid', axis=1, tiled=True)  19 us
  transfers between devices with their start and end apart: 18, of which 5 were waited for; matrix products, arithmetic and copies ran while one was open for 16% of the time, Pallas kernels for 0%

commit v1 on v0

v1 whole, which is shorter than its diff:
```python
import jax
import jax.numpy as jnp
from jax import lax
from jax.sharding import PartitionSpec as P

LEARNING_RATE = 0.5
LINK_SCALE = 8192.0


def swapped(value, axis, distance):
    pairs = [(source, source ^ distance) for source in range(lax.axis_size(axis))]
    return lax.ppermute(value, axis, pairs)


def gelu_tanh(value):
    return jax.nn.gelu(value, approximate=True)


def contract_cols(left, right):
    return lax.dot_general(
        left, right, (((1,), (1,)), ((), ())), preferred_element_type=jnp.float32
    )


def contract_rows(left, right):
    return lax.dot_general(
        left, right, (((0,), (0,)), ((), ())), preferred_element_type=jnp.float32
    )


def to_link(value):
    return (value * LINK_SCALE).astype(jnp.float16)


def from_link(value):
    return value.astype(jnp.float32) * (1.0 / LINK_SCALE)


def factors(tokens, targets, weights, scale_model, scale_hidden):
    gate_half, up_half, down_half = weights
    gate_value = contract_cols(tokens, gate_half) * scale_model
    up_value = contract_cols(tokens, up_half) * scale_model
    activated, gelu_back = jax.vjp(gelu_tanh, gate_value)
    hidden = (activated * up_value).astype(jnp.bfloat16)
    partial_out = (
        jnp.dot(hidden, down_half, preferred_element_type=jnp.float32) * scale_hidden
    )
    output = lax.psum(partial_out, "hid")
    residual = (output - targets.astype(jnp.float32)).astype(jnp.bfloat16)
    hidden_grad = contract_cols(residual, down_half) * scale_hidden
    gate_grad = gelu_back(hidden_grad * up_value)[0].astype(jnp.bfloat16)
    up_grad = (hidden_grad * activated).astype(jnp.bfloat16)
    return gate_grad, up_grad, hidden, residual


def local(tokens, targets, w_gate, w_up, w_down):
    hid = lax.axis_size("hid")
    features = w_gate.shape[2]
    rows = w_gate.shape[1]
    scale_model = float(features) ** (-0.5)
    scale_hidden = float(rows * hid) ** (-0.5)
    scales = (scale_model, scale_model, scale_hidden)
    core = lax.rem(lax.axis_index("rep"), 2)
    weights = (w_gate[0], w_up[0], w_down[0])
    half = rows // 2

    all_tokens = lax.all_gather(tokens, "hid", axis=1, tiled=True)
    all_targets = lax.all_gather(targets, "hid", axis=1, tiled=True)

    means = []
    for weight in weights:
        theirs = swapped(to_link(weight), "rep", 1)
        means.append((weight + from_link(theirs)) * 0.5)
    far = []
    for mean in means:
        part = lax.dynamic_slice_in_dim(mean, core * half, half, 0)
        far.append(swapped(to_link(part), "rep", 2))
    near = [swapped(part, "rep", 1) for part in far]

    own = factors(
        all_tokens[0],
        all_targets[0],
        tuple(w.astype(jnp.bfloat16) for w in weights),
        scale_model,
        scale_hidden,
    )
    own = (*own, all_tokens[0])
    pair = swapped(own, "rep", 1)
    far_zero = swapped(own, "rep", 2)
    near_zero = swapped(far_zero, "rep", 1)
    stepped = []
    for index in range(3):
        right = 3 if index == 2 else 4
        grad = contract_rows(
            jnp.concatenate([own[index], pair[index]]),
            jnp.concatenate([own[right], pair[right]]),
        )
        stepped.append(
            means[index] - grad * (0.5 * LEARNING_RATE * scales[index])
        )

    mine = factors(
        all_tokens[1],
        all_targets[1],
        tuple(w.astype(jnp.bfloat16) for w in stepped),
        scale_model,
        scale_hidden,
    )
    mine = (*mine, all_tokens[1])
    far_one = swapped(mine, "rep", 2)
    out = []
    for index in range(3):
        right = 3 if index == 2 else 4
        grad = contract_rows(
            jnp.concatenate(
                [far_zero[index], near_zero[index], mine[index] * 2, far_one[index] * 2]
            ),
            jnp.concatenate(
                [far_zero[right], near_zero[right], mine[right], far_one[right]]
            ),
        )
        low = jnp.where(core == 0, far[index], near[index])
        high = jnp.where(core == 0, near[index], far[index])
        other = from_link(jnp.concatenate([low, high]))
        out.append(
            ((stepped[index] + other) * 0.5
             - grad * (0.25 * LEARNING_RATE * scales[index]))[None]
        )
    return tuple(out)


def solution(mesh):
    rows = P(None, ("rep", "hid"), None)
    weight = P("rep", "hid", None)
    return jax.shard_map(
        local,
        mesh=mesh,
        in_specs=(rows, rows, weight, weight, weight),
        out_specs=(weight, weight, weight),
        check_vma=False,
    )
```

time: 699 us -> 357 us (0.51)
  waiting for transfers between devices: 510 us -> 154 us
  other arithmetic: 2.23 us -> 60.3 us
  matrix products: 117 us -> 61 us
  starting transfers between devices: 11.1 us -> 19.1 us
    ppermute x16 -> x29, waiting for transfers between devices: 451 us -> 118 us  [swapped(): return lax.ppermute(value, axis, pairs)]
    dot_general x12 -> x6, matrix products: 80.9 us -> 31.6 us  [contract_rows(): lax.dot_general(left, right, (((0,), (0,)), ((), ())), preferred_element_...]
    convert_element_type x2 -> x8, other arithmetic: 2.23 us -> 31.9 us  [the longest x6 29.5 us: to_link(): return (value * LINK_SCALE).astype(jnp.float16)]
    psum x2, waiting for transfers between devices: 59 us -> 36.1 us  [factors(): output = lax.psum(partial_out, 'hid')]
    mul x0 -> x6, other arithmetic: none -> 22.4 us  [the longest x3 18.9 us: local(): means.append((weight + from_link(theirs)) * 0.5)]
    ppermute x16 -> x29, starting transfers between devices: 11 us -> 19 us  [swapped(): return lax.ppermute(value, axis, pairs)]
  transfers between devices with their start and end apart: 18 -> 31, of which waited for: 5 -> 8; matrix products, arithmetic and copies ran while one was open for 16% -> 32% of each run, Pallas kernels for 0% -> 0%
where the time goes in v1:
time: 357 us; the launch traced here: 356 us
  waiting for transfers between devices  154 us (43%)
  matrix products  61 us (17%)
  other arithmetic  60.3 us (17%)
  blocking collectives  39.5 us (11%)
  starting transfers between devices  19.1 us (5%)
  between operations  14.6 us (4%)
  local copies, waits for them, and re-layouts  7.69 us (2%)
    ppermute x29, waiting for transfers between devices, swapped(): return lax.ppermute(value, axis, pairs)  118 us
    psum x2, waiting for transfers between devices, factors(): output = lax.psum(partial_out, 'hid')  36.1 us
    dot_general x6, matrix products, contract_rows(): lax.dot_general(left, right, (((0,), (0,)), ((), ())), preferred_element_...  31.6 us
    convert_element_type x6, other arithmetic, to_link(): return (value * LINK_SCALE).astype(jnp.float16)  29.5 us
    dot_general x6, matrix products, contract_cols(): lax.dot_general(left, right, (((1,), (1,)), ((), ())), preferred_element_...  24.1 us
    all_gather x1, blocking collectives, local(): all_targets = lax.all_gather(targets, 'hid', axis=1, tiled=True)  21.2 us
    ppermute x29, starting transfers between devices, swapped(): return lax.ppermute(value, axis, pairs)  19 us
    mul x3, other arithmetic, local(): means.append((weight + from_link(theirs)) * 0.5)  18.9 us
  transfers between devices with their start and end apart: 31, of which 8 were waited for; matrix products, arithmetic and copies ran while one was open for 32% of the time, Pallas kernels for 0%

profile of v1, /device:TPU:0, one launch (start us, length us, event | category | flops | bytes accessed | tf_op | source)
XLA Modules:
  0.0 356.1 jit_solution(10129658746916096144)
XLA Ops:
  7.2 18.4 %all_gather.6 = bf16[2,128,1152]{2,1,0:T(8,128)(2,1)S(1)} all-gather(bf16[2,32,1152]{2,1,0:T(8,128)(2,1)} %param.5), channel_id=1, replica_groups=mesh['rep'=8,'hid'=4] {'hid'}, dimensions={1}, use_global_device_ids=true | all-gather | bytes 737280 | tf_op jit(solution)/shard_map/all_gather | solution.py:67
  28.1 5.1 %fusion.25 = f32[128,1728]{0,1:T(8,128)S(1)} fusion(f32[1,1728,1152]{2,1,0:T(8,128)} %param.7, bf16[2,128,1152]{2,1,0:T(8,128)(2,1)S(1)} %all_gather.6), kind=kOutput, calls=%fused_computation.42 | convolution fusion | flops 511819776 | bytes 9142272 | tf_op jit(solution)/shard_map/dot_general | solution.py:20
  38.1 6.2 %fusion.5 = f16[1728,1152]{1,0:T(8,128)(2,1)} fusion(f32[1,1728,1152]{2,1,0:T(8,128)} %param.9), kind=kLoop, calls=%fused_computation.16 | loop fusion | flops 3981312 | bytes 11943936 | tf_op jit(solution)/shard_map/convert_element_type | solution.py:32
  44.3 6.2 %fusion.3 = f16[1728,1152]{1,0:T(8,128)(2,1)} fusion(f32[1,1728,1152]{2,1,0:T(8,128)} %param.8), kind=kLoop, calls=%fused_computation.11 | loop fusion | flops 3981312 | bytes 11943936 | tf_op jit(solution)/shard_map/convert_element_type | solution.py:32
  54.0 21.2 %all_gather.7 = bf16[2,128,1152]{2,1,0:T(8,128)(2,1)S(1)} all-gather(bf16[2,32,1152]{2,1,0:T(8,128)(2,1)S(1)} %copy-done.23), channel_id=1, replica_groups=mesh['rep'=8,'hid'=4] {'hid'}, dimensions={1}, use_global_device_ids=true | all-gather | bytes 737280 | tf_op jit(solution)/shard_map/all_gather | solution.py:68
  75.2 6.2 %all-reduce.3.cloned.1.call-done = f32[128,1152]{1,0:T(8,128)} async-done(((f32[128,1152]{1,0:T(8,128)}), f32[128,1152]{1,0:T(8,128)}) %all-reduce.3.cloned.1.call-update) | async-done | bytes 589840 | tf_op jit(solution)/shard_map/psum | solution.py:48
  82.5 6.2 %multiply_convert_fusion.5 = (bf16[128,1728]{0,1:T(8,128)(2,1)}, bf16[128,1728]{0,1:T(8,128)(2,1)}) fusion(f32[128,1728]{0,1:T(8,128)S(1)} %fusion.25, f32[128,1728]{0,1:T(8,128)S(1)} %get-tuple-element.22, bf16[128,1152]{1,0:T(8,128)(2,1)S(1)} %fusion.94, f32[1,1728,1152]{2,1,0:T(8,128)} %param.9), kind=kOutput, calls=%fused_computation.114 | convolution fusion | flops 515137536 | bytes 10911744 | tf_op jit(solution)/shard_map/dot_general | solution.py:20
  88.8 8.7 %fusion.6 = f32[1728,1152]{1,0:T(8,128)} fusion(f32[1,1728,1152]{2,1,0:T(8,128)} %param.9, f16[1728,1152]{1,0:T(8,128)(2,1)} %collective-permute-done.9), kind=kLoop, calls=%fused_computation.17 | loop fusion | flops 7962624 | bytes 19906560 | tf_op jit(solution)/shard_map/mul | solution.py:73
  98.2 6.9 %fusion.4 = f32[1728,1152]{1,0:T(8,128)} fusion(f32[1,1728,1152]{2,1,0:T(8,128)S(1)} %bitcast.93, f16[1728,1152]{1,0:T(8,128)(2,1)} %collective-permute-done.7), kind=kLoop, calls=%fused_computation.12 | loop fusion | flops 7962624 | bytes 19906560 | tf_op jit(solution)/shard_map/mul | solution.py:73
  105.2 3.3 fusion.8
  108.5 6.7 %multiply_convert_fusion.1 = f16[864,1152]{1,0:T(8,128)(2,1)} fusion(f32[1728,1152]{1,0:T(8,128)} %fusion.4, s32[]{:T(128)S(6)} %select_n.34), kind=kLoop, calls=%fused_computation.30 | loop fusion | flops 1990656 | bytes 5971972 | tf_op jit(solution)/shard_map/convert_element_type | solution.py:32
  133.9 3.2 copy-done.1
  139.8 3.9 %multiply_convert_fusion.2 = f16[864,1152]{1,0:T(8,128)(2,1)} fusion(f32[1728,1152]{1,0:T(8,128)} %copy-done.3, s32[]{:T(128)S(6)} %select_n.34), kind=kLoop, calls=%fused_computation.35 | loop fusion | flops 1990656 | bytes 5971972 | tf_op jit(solution)/shard_map/convert_element_type | solution.py:32
  145.1 3.8 %multiply_convert_fusion = f16[864,1152]{1,0:T(8,128)(2,1)} fusion(f32[1728,1152]{1,0:T(8,128)} %fusion.6, s32[]{:T(128)S(6)} %select_n.34), kind=kLoop, calls=%fused_computation.29 | loop fusion | flops 1990656 | bytes 5971972 | tf_op jit(solution)/shard_map/convert_element_type | solution.py:32
  148.9 29.9 %all-reduce.5.cloned.1.call-done = f32[128,1152]{1,0:T(8,128)} async-done(((f32[128,1152]{1,0:T(8,128)}), f32[128,1152]{1,0:T(8,128)}) %all-reduce.5.cloned.1.call-update) | async-done | bytes 589840 | tf_op jit(solution)/shard_map/psum | solution.py:48
  180.2 6.3 %broadcast_multiply_fusion.3 = (bf16[128,1728]{0,1:T(8,128)(2,1)}, bf16[128,1728]{0,1:T(8,128)(2,1)S(1)}, bf16[128,1728]{0,1:T(8,128)(2,1)}, bf16[128,1728]{0,1:T(8,128)(2,1)S(1)}) fusion(f32[128,1728]{0,1:T(8,128)S(1)} %copy-done.6, f32[128,1728]{0,1:T(8,128)S(1)} %get-tuple-element.23, bf16[128,1152]{1,0:T(8,128)(2,1)S(1)} %fusion.93, ...), kind=kOutput, calls=%fused_computation.133 | convolution fusion | flops 517570560 | bytes 11796480 | tf_op jit(solution)/shard_map/dot_general | solution.py:20
  192.0 81.3 %collective-permute-done.20 = bf16[128,1728]{0,1:T(8,128)(2,1)S(1)} collective-permute-done((bf16[128,1728]{0,1:T(8,128)(2,1)S(1)}, bf16[128,1728]{0,1:T(8,128)(2,1)S(1)}, u32[]{:S(2)}, u32[]{:S(2)}) %collective-permute-start.20) | collective-permute-done | bytes 442400 | tf_op jit(solution)/shard_map/ppermute | solution.py:12
  276.0 6.8 %collective-permute-done.23 = bf16[128,1728]{0,1:T(8,128)(2,1)} collective-permute-done((bf16[128,1728]{0,1:T(8,128)(2,1)}, bf16[128,1728]{0,1:T(8,128)(2,1)}, u32[]{:S(2)}, u32[]{:S(2)}) %collective-permute-start.23) | collective-permute-done | bytes 442400 | tf_op jit(solution)/shard_map/ppermute | solution.py:12
  282.9 9.0 %collective-permute-done.12 = bf16[128,1728]{0,1:T(8,128)(2,1)S(1)} collective-permute-done((bf16[128,1728]{0,1:T(8,128)(2,1)S(1)}, bf16[128,1728]{0,1:T(8,128)(2,1)S(1)}, u32[]{:S(2)}, u32[]{:S(2)}) %collective-permute-start.12) | collective-permute-done | bytes 442400 | tf_op jit(solution)/shard_map/ppermute | solution.py:12
  294.7 10.2 %collective-permute-done.18 = bf16[128,1728]{0,1:T(8,128)(2,1)S(1)} collective-permute-done((bf16[128,1728]{0,1:T(8,128)(2,1)S(1)}, bf16[128,1728]{0,1:T(8,128)(2,1)S(1)}, u32[]{:S(2)}, u32[]{:S(2)}) %collective-permute-start.18) | collective-permute-done | bytes 442400 | tf_op jit(solution)/shard_map/ppermute | solution.py:12
  311.3 8.2 %collective-permute-done.5 = bf16[128,1728]{0,1:T(8,128)(2,1)} collective-permute-done((bf16[128,1728]{0,1:T(8,128)(2,1)S(1)}, bf16[128,1728]{0,1:T(8,128)(2,1)}, u32[]{:S(2)}, u32[]{:S(2)}) %collective-permute-start.5) | collective-permute-done | bytes 442400 | tf_op jit(solution)/shard_map/ppermute | solution.py:12
  320.2 8.4 %subtract_bitcast_fusion.1 = f32[1,1728,1152]{2,1,0:T(8,128)} fusion(f32[1728,1152]{1,0:T(8,128)S(1)} %bitcast.107, f16[864,1152]{1,0:T(8,128)(2,1)S(1)} %get-tuple-element.12, f16[864,1152]{1,0:T(8,128)(2,1)S(1)} %get-tuple-element.11, bf16[128,1728]{0,1:T(8,128)(2,1)} %broadcast_multiply_fusion.2, bf16[128,1728]{0,1:T(8,128)(2,1)} %get-tuple-element.5, ...), kind=kOutput, calls=%fused_computation.23 | convolution fusion | flops 2064162816 | bytes 22855680 | tf_op jit(solution)/shard_map/dot_general | solution.py:26
  332.9 7.7 %subtract_bitcast_fusion.2 = f32[1,1728,1152]{2,1,0:T(8,128)} fusion(f32[1728,1152]{1,0:T(8,128)S(1)} %bitcast.101, f16[864,1152]{1,0:T(8,128)(2,1)S(1)} %get-tuple-element.14, f16[864,1152]{1,0:T(8,128)(2,1)S(1)} %get-tuple-element.13, bf16[128,1728]{0,1:T(8,128)(2,1)S(1)} %copy-done.19, bf16[128,1728]{0,1:T(8,128)(2,1)S(1)} %copy-done.20, ...), kind=kOutput, calls=%fused_computation.24 | convolution fusion | flops 2064162816 | bytes 22855680 | tf_op jit(solution)/shard_map/dot_general | solution.py:26
  341.7 7.6 %subtract_bitcast_fusion = f32[1,1728,1152]{2,1,0:T(8,128)} fusion(f32[1728,1152]{1,0:T(8,128)S(1)} %bitcast.99, f16[864,1152]{1,0:T(8,128)(2,1)S(1)} %get-tuple-element.10, f16[864,1152]{1,0:T(8,128)(2,1)S(1)} %get-tuple-element.9, bf16[128,1728]{0,1:T(8,128)(2,1)S(1)} %copy-done.18, bf16[128,1728]{0,1:T(8,128)(2,1)S(1)} %copy-done.21, ...), kind=kOutput, calls=%fused_computation.22 | convolution fusion | flops 2064162816 | bytes 22855680 | tf_op jit(solution)/shard_map/dot_general | solution.py:26
  (171 shorter events, 60.2 us)
Async XLA Ops:
  7.2 74.2 %all-reduce.3.cloned.1.call-start = ((), (), s32[]{:S(2)}) async-start(), calls=%async_computation | async-start | bytes 1179648 | tf_op jit(solution)/shard_map/psum | solution.py:48
  26.6 88.7 %collective-permute-start.2 = (bf16[128,1152]{1,0:T(8,128)(2,1)}, bf16[128,1152]{1,0:T(8,128)(2,1)}, u32[]{:S(2)}, u32[]{:S(2)}) collective-permute-start(bf16[128,1152]{1,0:T(8,128)(2,1)} %get-tuple-element.20), channel_id=1, source_target_pairs={{0,4},{4,0},{8,12},{12,8},{16,20},{20,16},{24,28},{28,24},{1,5},{5... | collective-permute-start | bytes 884744 | tf_op jit(solution)/shard_map/ppermute | solution.py:12
  26.6 163.9 %collective-permute-start.13 = (bf16[128,1152]{1,0:T(8,128)(2,1)}, bf16[128,1152]{1,0:T(8,128)(2,1)}, u32[]{:S(2)}, u32[]{:S(2)}) collective-permute-start(bf16[128,1152]{1,0:T(8,128)(2,1)} %get-tuple-element.20), channel_id=1, source_target_pairs={{0,8},{4,12},{8,0},{12,4},{16,24},{20,28},{24,16},{28,20},{1,9},{5... | collective-permute-start | bytes 884744 | tf_op jit(solution)/shard_map/ppermute | solution.py:12
  38.0 140.7 %all-reduce.5.cloned.1.call-start = ((), (), s32[]{:S(2)}) async-start(), calls=%async_computation.1 | async-start | bytes 1179648 | tf_op jit(solution)/shard_map/psum | solution.py:48
  44.3 44.5 %collective-permute-start.9 = (f16[1728,1152]{1,0:T(8,128)(2,1)}, f16[1728,1152]{1,0:T(8,128)(2,1)}, u32[]{:S(2)}, u32[]{:S(2)}) collective-permute-start(f16[1728,1152]{1,0:T(8,128)(2,1)} %fusion.5), channel_id=1, source_target_pairs={{0,4},{4,0},{8,12},{12,8},{16,20},{20,16},{24,28},{28,24},{1,5},{5... | collective-permute-start | bytes 11943944 | tf_op jit(solution)/shard_map/ppermute | solution.py:12
  50.4 47.1 %collective-permute-start.7 = (f16[1728,1152]{1,0:T(8,128)(2,1)}, f16[1728,1152]{1,0:T(8,128)(2,1)}, u32[]{:S(2)}, u32[]{:S(2)}) collective-permute-start(f16[1728,1152]{1,0:T(8,128)(2,1)} %fusion.3), channel_id=1, source_target_pairs={{0,4},{4,0},{8,12},{12,8},{16,20},{20,16},{24,28},{28,24},{1,5},{5... | collective-permute-start | bytes 11943944 | tf_op jit(solution)/shard_map/ppermute | solution.py:12
  54.0 51.2 %collective-permute-start = (f16[1728,1152]{1,0:T(8,128)(2,1)}, f16[1728,1152]{1,0:T(8,128)(2,1)}, u32[]{:S(2)}, u32[]{:S(2)}) collective-permute-start(f16[1728,1152]{1,0:T(8,128)(2,1)} %fusion.7), channel_id=1, source_target_pairs={{0,4},{4,0},{8,12},{12,8},{16,20},{20,16},{24,28},{28,24},{1,5},{5... | collective-permute-start | bytes 11943944 | tf_op jit(solution)/shard_map/ppermute | solution.py:12
  88.8 41.8 %collective-permute-start.10 = (bf16[128,1728]{0,1:T(8,128)(2,1)}, bf16[128,1728]{0,1:T(8,128)(2,1)}, u32[]{:S(2)}, u32[]{:S(2)}) collective-permute-start(bf16[128,1728]{0,1:T(8,128)(2,1)} %get-tuple-element.21), channel_id=1, source_target_pairs={{0,4},{4,0},{8,12},{12,8},{16,20},{20,16},{24,28},{28,24},{1,5},{5... | collective-permute-start | bytes 1327112 | tf_op jit(solution)/shard_map/ppermute | solution.py:12
  97.6 89.0 %collective-permute-start.15 = (bf16[128,1152]{1,0:T(8,128)(2,1)}, bf16[128,1152]{1,0:T(8,128)(2,1)}, u32[]{:S(2)}, u32[]{:S(2)}) collective-permute-start(bf16[128,1152]{1,0:T(8,128)(2,1)} %get-tuple-element.19), channel_id=1, source_target_pairs={{0,8},{4,12},{8,0},{12,4},{16,24},{20,28},{24,16},{28,20},{1,9},{5... | collective-permute-start | bytes 884744 | tf_op jit(solution)/shard_map/ppermute | solution.py:12
  115.3 15.8 %collective-permute-start.11 = (bf16[128,1152]{1,0:T(8,128)(2,1)S(1)}, bf16[128,1152]{1,0:T(8,128)(2,1)S(1)}, u32[]{:S(2)}, u32[]{:S(2)}) collective-permute-start(bf16[128,1152]{1,0:T(8,128)(2,1)S(1)} %fusion.94), channel_id=1, source_target_pairs={{0,4},{4,0},{8,12},{12,8},{16,20},{20,16},{24,28},{28,24},{1,5},{5... | collective-permute-start | bytes 884744 | tf_op jit(solution)/shard_map/ppermute | solution.py:12
  122.6 57.4 %collective-permute-start.16 = (f16[864,1152]{1,0:T(8,128)(2,1)}, f16[864,1152]{1,0:T(8,128)(2,1)}, u32[]{:S(2)}, u32[]{:S(2)}) collective-permute-start(f16[864,1152]{1,0:T(8,128)(2,1)} %multiply_convert_fusion.1), channel_id=1, source_target_pairs={{0,8},{4,12},{8,0},{12,4},{16,24},{20,28},{24,16},{28,20},{1,9},{5... | collective-permute-start | bytes 5971976 | tf_op jit(solution)/shard_map/ppermute | solution.py:12
  130.5 57.6 %collective-permute-start.25 = (bf16[128,1728]{0,1:T(8,128)(2,1)}, bf16[128,1728]{0,1:T(8,128)(2,1)}, u32[]{:S(2)}, u32[]{:S(2)}) collective-permute-start(bf16[128,1728]{0,1:T(8,128)(2,1)} %get-tuple-element.4), channel_id=1, source_target_pairs={{0,8},{4,12},{8,0},{12,4},{16,24},{20,28},{24,16},{28,20},{1,9},{5... | collective-permute-start | bytes 1327112 | tf_op jit(solution)/shard_map/ppermute | solution.py:12
  143.6 150.0 %collective-permute-start.3 = (f16[864,1152]{1,0:T(8,128)(2,1)}, f16[864,1152]{1,0:T(8,128)(2,1)}, u32[]{:S(2)}, u32[]{:S(2)}) collective-permute-start(f16[864,1152]{1,0:T(8,128)(2,1)} %multiply_convert_fusion.2), channel_id=1, source_target_pairs={{0,8},{4,12},{8,0},{12,4},{16,24},{20,28},{24,16},{28,20},{1,9},{5... | collective-permute-start | bytes 5971976 | tf_op jit(solution)/shard_map/ppermute | solution.py:12
  180.1 126.6 %collective-permute-start.17 = (f16[864,1152]{1,0:T(8,128)(2,1)}, f16[864,1152]{1,0:T(8,128)(2,1)S(1)}, u32[]{:S(2)}, u32[]{:S(2)}) collective-permute-start(f16[864,1152]{1,0:T(8,128)(2,1)} %collective-permute-done.16), channel_id=1, source_target_pairs={{0,4},{4,0},{8,12},{12,8},{16,20},{20,16},{24,28},{28,24},{1,5},{5... | collective-permute-start | bytes 5971976 | tf_op jit(solution)/shard_map/ppermute | solution.py:12
  186.6 133.5 %collective-permute-start.21 = (f16[864,1152]{1,0:T(8,128)(2,1)S(1)}, f16[864,1152]{1,0:T(8,128)(2,1)S(1)}, u32[]{:S(2)}, u32[]{:S(2)}) collective-permute-start(f16[864,1152]{1,0:T(8,128)(2,1)S(1)} %copy-done.11), channel_id=1, source_target_pairs={{0,8},{4,12},{8,0},{12,4},{16,24},{20,28},{24,16},{28,20},{1,9},{5... | collective-permute-start | bytes 5971976 | tf_op jit(solution)/shard_map/ppermute | solution.py:12
  188.1 85.2 %collective-permute-start.20 = (bf16[128,1728]{0,1:T(8,128)(2,1)S(1)}, bf16[128,1728]{0,1:T(8,128)(2,1)S(1)}, u32[]{:S(2)}, u32[]{:S(2)}) collective-permute-start(bf16[128,1728]{0,1:T(8,128)(2,1)S(1)} %get-tuple-element.6), channel_id=1, source_target_pairs={{0,8},{4,12},{8,0},{12,4},{16,24},{20,28},{24,16},{28,20},{1,9},{5... | collective-permute-start | bytes 1327112 | tf_op jit(solution)/shard_map/ppermute | solution.py:12
  190.5 92.4 %collective-permute-start.23 = (bf16[128,1728]{0,1:T(8,128)(2,1)}, bf16[128,1728]{0,1:T(8,128)(2,1)}, u32[]{:S(2)}, u32[]{:S(2)}) collective-permute-start(bf16[128,1728]{0,1:T(8,128)(2,1)} %get-tuple-element.21), channel_id=1, source_target_pairs={{0,8},{4,12},{8,0},{12,4},{16,24},{20,28},{24,16},{28,20},{1,9},{5... | collective-permute-start | bytes 1327112 | tf_op jit(solution)/shard_map/ppermute | solution.py:12
  273.3 18.6 %collective-permute-start.12 = (bf16[128,1728]{0,1:T(8,128)(2,1)S(1)}, bf16[128,1728]{0,1:T(8,128)(2,1)S(1)}, u32[]{:S(2)}, u32[]{:S(2)}) collective-permute-start(bf16[128,1728]{0,1:T(8,128)(2,1)S(1)} %get-tuple-element.16), channel_id=1, source_target_pairs={{0,8},{4,12},{8,0},{12,4},{16,24},{20,28},{24,16},{28,20},{1,9},{5... | collective-permute-start | bytes 1327112 | tf_op jit(solution)/shard_map/ppermute | solution.py:12
  293.6 35.0 %collective-permute-start.4 = (f16[864,1152]{1,0:T(8,128)(2,1)}, f16[864,1152]{1,0:T(8,128)(2,1)S(1)}, u32[]{:S(2)}, u32[]{:S(2)}) collective-permute-start(f16[864,1152]{1,0:T(8,128)(2,1)} %collective-permute-done.3), channel_id=1, source_target_pairs={{0,4},{4,0},{8,12},{12,8},{16,20},{20,16},{24,28},{28,24},{1,5},{5... | collective-permute-start | bytes 5971976 | tf_op jit(solution)/shard_map/ppermute | solution.py:12
  294.4 17.0 %collective-permute-start.26 = (bf16[128,1152]{1,0:T(8,128)(2,1)S(1)}, bf16[128,1152]{1,0:T(8,128)(2,1)}, u32[]{:S(2)}, u32[]{:S(2)}) collective-permute-start(bf16[128,1152]{1,0:T(8,128)(2,1)S(1)} %fusion.94), channel_id=1, source_target_pairs={{0,8},{4,12},{8,0},{12,4},{16,24},{20,28},{24,16},{28,20},{1,9},{5... | collective-permute-start | bytes 884744 | tf_op jit(solution)/shard_map/ppermute | solution.py:12
  304.9 14.6 %collective-permute-start.5 = (bf16[128,1728]{0,1:T(8,128)(2,1)S(1)}, bf16[128,1728]{0,1:T(8,128)(2,1)}, u32[]{:S(2)}, u32[]{:S(2)}) collective-permute-start(bf16[128,1728]{0,1:T(8,128)(2,1)S(1)} %copy-done.13), channel_id=1, source_target_pairs={{0,8},{4,12},{8,0},{12,4},{16,24},{20,28},{24,16},{28,20},{1,9},{5... | collective-permute-start | bytes 1327112 | tf_op jit(solution)/shard_map/ppermute | solution.py:12
  311.3 30.2 %collective-permute-start.24 = (bf16[128,1728]{0,1:T(8,128)(2,1)}, bf16[128,1728]{0,1:T(8,128)(2,1)}, u32[]{:S(2)}, u32[]{:S(2)}) collective-permute-start(bf16[128,1728]{0,1:T(8,128)(2,1)} %collective-permute-done.23), channel_id=1, source_target_pairs={{0,4},{4,0},{8,12},{12,8},{16,20},{20,16},{24,28},{28,24},{1,5},{5... | collective-permute-start | bytes 1327112 | tf_op jit(solution)/shard_map/ppermute | solution.py:12
  319.5 22.0 %collective-permute-start.27 = (bf16[128,1152]{1,0:T(8,128)(2,1)}, bf16[128,1152]{1,0:T(8,128)(2,1)}, u32[]{:S(2)}, u32[]{:S(2)}) collective-permute-start(bf16[128,1152]{1,0:T(8,128)(2,1)} %collective-permute-done.26), channel_id=1, source_target_pairs={{0,4},{4,0},{8,12},{12,8},{16,20},{20,16},{24,28},{28,24},{1,5},{5... | collective-permute-start | bytes 884744 | tf_op jit(solution)/shard_map/ppermute | solution.py:12
  320.1 20.5 %collective-permute-start.22 = (f16[864,1152]{1,0:T(8,128)(2,1)S(1)}, f16[864,1152]{1,0:T(8,128)(2,1)S(1)}, u32[]{:S(2)}, u32[]{:S(2)}) collective-permute-start(f16[864,1152]{1,0:T(8,128)(2,1)S(1)} %collective-permute-done.21), channel_id=1, source_target_pairs={{0,4},{4,0},{8,12},{12,8},{16,20},{20,16},{24,28},{28,24},{1,5},{5... | collective-permute-start | bytes 5971976 | tf_op jit(solution)/shard_map/ppermute | solution.py:12
  (51 other events, 961.1 us)
Sparse Core Ops, SparseCore 0:
  38.2 43.1 all-reduce.2
  139.9 38.8 all-reduce.4

commit v2 on v1

v2 whole, which is shorter than its diff:
```python
import jax
import jax.numpy as jnp
from jax import lax
from jax.sharding import PartitionSpec as P

LEARNING_RATE = 0.5
LINK_SCALE = 8192.0


def swapped(value, axis, distance):
    pairs = [(source, source ^ distance) for source in range(lax.axis_size(axis))]
    return lax.ppermute(value, axis, pairs)


def gathered(value, axis, dim):
    size = lax.axis_size(axis)
    me = lax.axis_index(axis)
    shards = [value]
    for shift in range(1, size):
        pairs = [(source, (source - shift) % size) for source in range(size)]
        shards.append(lax.ppermute(value, axis, pairs))
    twice = jnp.concatenate(shards + shards[:-1], axis=dim)
    width = value.shape[dim]
    start = lax.rem(size - me, size) * width
    return lax.dynamic_slice_in_dim(twice, start, size * width, dim)


def gelu_tanh(value):
    return jax.nn.gelu(value, approximate=True)


def contract_cols(left, right):
    return lax.dot_general(
        left, right, (((1,), (1,)), ((), ())), preferred_element_type=jnp.float32
    )


def contract_rows(left, right):
    return lax.dot_general(
        left, right, (((0,), (0,)), ((), ())), preferred_element_type=jnp.float32
    )


def to_link(value):
    return (value * LINK_SCALE).astype(jnp.float16)


def from_link(value):
    return value.astype(jnp.float32) * (1.0 / LINK_SCALE)


def in_order(core, own, other):
    low = jnp.where(core == 0, own, other)
    high = jnp.where(core == 0, other, own)
    return jnp.concatenate([low, high])


def factors(tokens, targets, weights, scale_model, scale_hidden):
    gate_half, up_half, down_half = weights
    gate_value = contract_cols(tokens, gate_half) * scale_model
    up_value = contract_cols(tokens, up_half) * scale_model
    activated, gelu_back = jax.vjp(gelu_tanh, gate_value)
    hidden = (activated * up_value).astype(jnp.bfloat16)
    partial_out = (
        jnp.dot(hidden, down_half, preferred_element_type=jnp.float32) * scale_hidden
    )
    output = lax.psum(partial_out, "hid")
    residual = (output - targets.astype(jnp.float32)).astype(jnp.bfloat16)
    hidden_grad = contract_cols(residual, down_half) * scale_hidden
    gate_grad = gelu_back(hidden_grad * up_value)[0].astype(jnp.bfloat16)
    up_grad = (hidden_grad * activated).astype(jnp.bfloat16)
    return jnp.concatenate([gate_grad, up_grad, hidden], axis=1), residual


def gradients(lefts, residuals, tokens):
    left = jnp.concatenate(lefts)
    rows = left.shape[1] // 3
    right = (jnp.concatenate(tokens),) * 2 + (jnp.concatenate(residuals),)
    return [
        contract_rows(left[:, index * rows : (index + 1) * rows], right[index])
        for index in range(3)
    ]


def local(tokens, targets, w_gate, w_up, w_down):
    hid = lax.axis_size("hid")
    features = w_gate.shape[2]
    rows = w_gate.shape[1]
    scale_model = float(features) ** (-0.5)
    scale_hidden = float(rows * hid) ** (-0.5)
    scales = (scale_model, scale_model, scale_hidden)
    core = lax.rem(lax.axis_index("rep"), 2)
    weights = (w_gate[0], w_up[0], w_down[0])
    half = rows // 2

    given = [
        to_link(lax.dynamic_slice_in_dim(w, (1 - core) * half, half, 0))
        for w in weights
    ]
    given, tokens, targets = lax.optimization_barrier((given, tokens, targets))
    taken = [swapped(part, "rep", 1) for part in given]
    both = gathered(jnp.concatenate([tokens, targets]), "hid", 1)
    means = [
        to_link(
            (lax.dynamic_slice_in_dim(w, core * half, half, 0) + from_link(part)) * 0.5
        )
        for w, part in zip(weights, taken)
    ]
    means, both = lax.optimization_barrier((means, both))
    far = [swapped(part, "rep", 2) for part in means]
    pair_means = [swapped(part, "rep", 1) for part in means]
    all_tokens, all_targets = both[:2], both[2:]
    pair_tokens = swapped(all_tokens, "rep", 1)
    far_tokens = gathered(swapped(tokens, "rep", 2), "hid", 1)
    near_tokens = swapped(far_tokens[0], "rep", 1)

    left, residual = factors(
        all_tokens[0],
        all_targets[0],
        tuple(w.astype(jnp.bfloat16) for w in weights),
        scale_model,
        scale_hidden,
    )
    pair_left, pair_residual = swapped((left, residual), "rep", 1)
    far_left, far_residual = swapped((left, residual), "rep", 2)
    near_left, near_residual = swapped((far_left, far_residual), "rep", 1)
    grads = gradients(
        (left, pair_left), (residual, pair_residual), (all_tokens[0], pair_tokens[0])
    )
    stepped = [
        from_link(in_order(core, mean, other)) - grad * (0.5 * LEARNING_RATE * scale)
        for mean, other, grad, scale in zip(means, pair_means, grads, scales)
    ]

    mine, my_residual = factors(
        all_tokens[1],
        all_targets[1],
        tuple(w.astype(jnp.bfloat16) for w in stepped),
        scale_model,
        scale_hidden,
    )
    theirs, their_residual = swapped((mine, my_residual), "rep", 2)
    near = [swapped(part, "rep", 1) for part in far]
    grads = gradients(
        (far_left, near_left), (far_residual, near_residual), (far_tokens[0], near_tokens)
    )
    base = [
        (weight + from_link(in_order(core, own, other))) * 0.5
        - grad * (0.25 * LEARNING_RATE * scale)
        for weight, own, other, grad, scale in zip(stepped, far, near, grads, scales)
    ]
    base = lax.optimization_barrier(base)
    grads = gradients(
        (mine, theirs), (my_residual, their_residual), (all_tokens[1], far_tokens[1])
    )
    return tuple(
        (weight - grad * (0.5 * LEARNING_RATE * scale))[None]
        for weight, grad, scale in zip(base, grads, scales)
    )


def solution(mesh):
    rows = P(None, ("rep", "hid"), None)
    weight = P("rep", "hid", None)
    return jax.shard_map(
        local,
        mesh=mesh,
        in_specs=(rows, rows, weight, weight, weight),
        out_specs=(weight, weight, weight),
        check_vma=False,
    )
```

time: 357 us -> 400 us (1.12); the launches traced: 356 us -> 394 us
  waiting for transfers between devices: 154 us -> 205 us
  blocking collectives: 39.5 us -> 0 us
  local copies, waits for them, and re-layouts: 7.69 us -> 25.7 us
  matrix products: 61 us -> 72.7 us
  other arithmetic: 60.3 us -> 49.4 us
  starting transfers between devices: 19.1 us -> 25.8 us
    all_gather x2 -> x0, blocking collectives: 39.5 us -> none  [the longest x1 21.2 us: local(): all_targets = lax.all_gather(targets, 'hid', axis=1, tiled=True)]
    ppermute x29 -> x23, waiting for transfers between devices: 118 us -> 145 us  [swapped(): return lax.ppermute(value, axis, pairs)]
    mul x6 -> x0, other arithmetic: 22.4 us -> none  [the longest x3 18.9 us: local(): means.append((weight + from_link(theirs)) * 0.5)]
    ppermute x0 -> x6, waiting for transfers between devices: none -> 21.8 us  [gathered(): shards.append(lax.ppermute(value, axis, pairs))]
    dot_general x6 -> x9, matrix products: 31.6 us -> 48 us  [contract_rows(): lax.dot_general(left, right, (((0,), (0,)), ((), ())), preferred_element_...]
    select_n x3 -> x6, other arithmetic: 6.07 us -> 22.4 us  [in_order(): low = jnp.where(core == 0, own, other)]
    ppermute x0 -> x6, starting transfers between devices: none -> 11.9 us  [gathered(): shards.append(lax.ppermute(value, axis, pairs))]
    unnamed x88 -> x106, local copies, waits for them, and re-layouts: 6.73 us -> 16.8 us
  transfers between devices with their start and end apart: 31 -> 31, of which waited for: 8 -> 7; matrix products, arithmetic and copies ran while one was open for 32% -> 33% of each run, Pallas kernels for 0% -> 0%
where the time goes in v2:
time: 400 us; the launch traced here: 394 us
  waiting for transfers between devices  205 us (51%)
  matrix products  72.7 us (18%)
  other arithmetic  49.4 us (12%)
  starting transfers between devices  25.8 us (6%)
  local copies, waits for them, and re-layouts  25.7 us (6%)
  between operations  15.2 us (4%)
    ppermute x23, waiting for transfers between devices, swapped(): return lax.ppermute(value, axis, pairs)  145 us
    dot_general x9, matrix products, contract_rows(): lax.dot_general(left, right, (((0,), (0,)), ((), ())), preferred_element_...  48 us
    psum x2, waiting for transfers between devices, factors(): output = lax.psum(partial_out, 'hid')  37.6 us
    select_n x6, other arithmetic, in_order(): low = jnp.where(core == 0, own, other)  22.4 us
    ppermute x6, waiting for transfers between devices, gathered(): shards.append(lax.ppermute(value, axis, pairs))  21.8 us
    convert_element_type x5, other arithmetic, to_link(): return (value * LINK_SCALE).astype(jnp.float16)  20.7 us
    dot_general x6, matrix products, contract_cols(): lax.dot_general(left, right, (((1,), (1,)), ((), ())), preferred_element_...  20.4 us
    unnamed x106, local copies, waits for them, and re-layouts  16.8 us
  transfers between devices with their start and end apart: 31, of which 7 were waited for; matrix products, arithmetic and copies ran while one was open for 33% of the time, Pallas kernels for 0%

profile of v2, /device:TPU:0, one launch (start us, length us, event | category | flops | bytes accessed | tf_op | source)
XLA Modules:
  0.0 393.5 jit_solution(12813445643496962101)
XLA Ops:
  11.0 5.5 %fusion.52 = (f16[864,1152]{1,0:T(8,128)(2,1)S(1)}, f16[864,1152]{1,0:T(8,128)(2,1)}) fusion(f32[1,1728,1152]{2,1,0:T(8,128)} %param.7, s32[]{:T(128)S(6)} %select_n.68, f32[1,1728,1152]{2,1,0:T(8,128)} %param.8), kind=kLoop, calls=%fused_computation.63 | loop fusion | flops 3981312 | bytes 11943940 | tf_op jit(solution)/shard_map/convert_element_type | solution.py:45
  17.9 5.0 %collective-permute-start.3 = (bf16[4,32,1152]{2,1,0:T(8,128)(2,1)}, bf16[4,32,1152]{2,1,0:T(8,128)(2,1)S(1)}, u32[]{:S(2)}, u32[]{:S(2)}) collective-permute-start(bf16[4,32,1152]{2,1,0:T(8,128)(2,1)} %get-tuple-element.47), channel_id=1, source_target_pairs={{0,3},{1,0},{2,1},{3,2},{4,7},{5,4},{6,5},{7,6},{8,11},{9,8},{10,9... | collective-permute-start | bytes 884744 | tf_op jit(solution)/shard_map/ppermute | solution.py:21
  25.5 5.3 %collective-permute-done.3 = bf16[4,32,1152]{2,1,0:T(8,128)(2,1)S(1)} collective-permute-done((bf16[4,32,1152]{2,1,0:T(8,128)(2,1)}, bf16[4,32,1152]{2,1,0:T(8,128)(2,1)S(1)}, u32[]{:S(2)}, u32[]{:S(2)}) %collective-permute-start.3) | collective-permute-done | bytes 294944 | tf_op jit(solution)/shard_map/ppermute | solution.py:21
  32.1 16.5 %collective-permute-done.4 = bf16[4,32,1152]{2,1,0:T(8,128)(2,1)S(1)} collective-permute-done((bf16[4,32,1152]{2,1,0:T(8,128)(2,1)}, bf16[4,32,1152]{2,1,0:T(8,128)(2,1)S(1)}, u32[]{:S(2)}, u32[]{:S(2)}) %collective-permute-start.4) | collective-permute-done | bytes 294944 | tf_op jit(solution)/shard_map/ppermute | solution.py:21
  49.3 5.7 %collective-permute-start.15 = (bf16[2,32,1152]{2,1,0:T(8,128)(2,1)}, bf16[2,32,1152]{2,1,0:T(8,128)(2,1)S(1)}, u32[]{:S(2)}, u32[]{:S(2)}) collective-permute-start(bf16[2,32,1152]{2,1,0:T(8,128)(2,1)} %collective-permute-done.13), channel_id=1, source_target_pairs={{0,2},{1,3},{2,0},{3,1},{4,6},{5,7},{6,4},{7,5},{8,10},{9,11},{10,... | collective-permute-start | bytes 442376 | tf_op jit(solution)/shard_map/ppermute | solution.py:21
  60.1 4.9 %fusion.25 = f16[864,1152]{1,0:T(8,128)(2,1)} fusion(f16[864,1152]{1,0:T(8,128)(2,1)} %collective-permute-done.2, f32[1,1728,1152]{2,1,0:T(8,128)} %param.9, s32[]{:T(128)S(6)} %select_n.67), kind=kLoop, calls=%fused_computation.39 | loop fusion | flops 4976640 | bytes 7962628 | tf_op jit(solution)/shard_map/convert_element_type | solution.py:45
  65.0 4.5 %fusion.27 = f16[864,1152]{1,0:T(8,128)(2,1)} fusion(f16[864,1152]{1,0:T(8,128)(2,1)S(1)} %collective-permute-done.1, f32[1,1728,1152]{2,1,0:T(8,128)} %param.8, s32[]{:T(128)S(6)} %select_n.67), kind=kLoop, calls=%fused_computation.42 | loop fusion | flops 4976640 | bytes 7962628 | tf_op jit(solution)/shard_map/convert_element_type | solution.py:45
  80.1 37.6 %all-reduce.3.cloned.1.call-done = f32[128,1152]{1,0:T(8,128)} async-done(((f32[128,1152]{1,0:T(8,128)}), f32[128,1152]{1,0:T(8,128)}) %all-reduce.3.cloned.1.call-update) | async-done | bytes 589840 | tf_op jit(solution)/shard_map/psum | solution.py:67
  118.8 5.1 %fusion.63 = (bf16[128,1728]{0,1:T(8,128)(2,1)S(1)}, bf16[128,1728]{0,1:T(8,128)(2,1)S(1)}) fusion(f32[128,1728]{0,1:T(8,128)S(1)} %fusion.37, f32[128,1728]{0,1:T(8,128)S(1)} %get-tuple-element.52, bf16[128,1152]{1,0:T(8,128)(2,1)S(1)} %fusion.90, f32[1,1728,1152]{2,1,0:T(8,128)} %param.9), kind=kOutput, calls=%fused_computation.92 | convolution fusion | flops 517128192 | bytes 10911744 | tf_op jit(solution)/shard_map/dot_general | solution.py:33
  135.3 3.9 collective-permute-done.22
  149.4 3.9 broadcast_select_fusion.3
  166.9 37.5 %collective-permute-done.11 = bf16[128,5184]{0,1:T(8,128)(2,1)} collective-permute-done((bf16[128,5184]{0,1:T(8,128)(2,1)}, bf16[128,5184]{0,1:T(8,128)(2,1)}, u32[]{:S(2)}, u32[]{:S(2)}) %collective-permute-start.11) | collective-permute-done | bytes 1327136 | tf_op jit(solution)/shard_map/ppermute | solution.py:12
  206.8 6.5 %fusion.70 = (bf16[128,1728]{0,1:T(8,128)(2,1)S(1)}, bf16[128,1728]{0,1:T(8,128)(2,1)S(1)}) fusion(f32[128,1728]{0,1:T(8,128)} %fusion.46, f32[128,1728]{0,1:T(8,128)} %get-tuple-element.54, bf16[128,1152]{1,0:T(8,128)(2,1)} %fusion.89, f32[1728,1152]{1,0:T(8,128)} %copy-done, f16[864,1152]{1,0:T(8,128)(2,1)} %copy-done.10, ...), kind=kOutput, calls=%fused_computation.99 | convolution fusion | flops 525090816 | bytes 14893056 | tf_op jit(solution)/shard_map/dot_general | solution.py:33
  216.4 73.3 %collective-permute-done.9 = f16[864,1152]{1,0:T(8,128)(2,1)} collective-permute-done((f16[864,1152]{1,0:T(8,128)(2,1)}, f16[864,1152]{1,0:T(8,128)(2,1)}, u32[]{:S(2)}, u32[]{:S(2)}) %collective-permute-start.9) | collective-permute-done | bytes 1990688 | tf_op jit(solution)/shard_map/ppermute | solution.py:12
  292.8 30.7 %collective-permute-done.25 = bf16[128,1152]{1,0:T(8,128)(2,1)} collective-permute-done((bf16[128,1152]{1,0:T(8,128)(2,1)S(1)}, bf16[128,1152]{1,0:T(8,128)(2,1)}, u32[]{:S(2)}, u32[]{:S(2)}) %collective-permute-start.25) | collective-permute-done | bytes 294944 | tf_op jit(solution)/shard_map/ppermute | solution.py:12
  327.4 5.1 %broadcast_select_fusion.5 = (f16[864,1152]{1,0:T(8,128)(2,1)}, f16[864,1152]{1,0:T(8,128)(2,1)}) fusion(f16[864,1152]{1,0:T(8,128)(2,1)} %collective-permute-done.19, f16[864,1152]{1,0:T(8,128)(2,1)} %collective-permute-done.20, pred[]{:T(512)S(6)} %eq.2), kind=kLoop, calls=%fused_computation.73 | loop fusion | flops 1990656 | bytes 7962625 | tf_op jit(solution)/shard_map/jit(_where)/select_n | solution.py:53
  332.6 4.7 %broadcast_select_fusion.9 = (f16[864,1152]{1,0:T(8,128)(2,1)}, f16[864,1152]{1,0:T(8,128)(2,1)}) fusion(f16[864,1152]{1,0:T(8,128)(2,1)} %collective-permute-done.9, f16[864,1152]{1,0:T(8,128)(2,1)S(1)} %collective-permute-done.10, pred[]{:T(512)S(6)} %eq.2), kind=kLoop, calls=%fused_computation.77 | loop fusion | flops 1990656 | bytes 7962625 | tf_op jit(solution)/shard_map/jit(_where)/select_n | solution.py:53
  337.3 10.1 %fusion.4 = f32[1728,1152]{1,0:T(8,128)} fusion(f32[1728,1152]{1,0:T(8,128)S(1)} %bitcast.88, f16[864,1152]{1,0:T(8,128)(2,1)} %get-tuple-element.34, f16[864,1152]{1,0:T(8,128)(2,1)} %get-tuple-element.33, f16[864,1152]{1,0:T(8,128)(2,1)} %copy-done.6, f16[864,1152]{1,0:T(8,128)(2,1)S(1)} %copy-done.5, bf16[256,5184]{0,1:T(8,128)(2,1)} %copy-done.24, ...), kind=kOutput, calls=%fused_computation.10 | convolution fusion | flops 1042292736 | bytes 25362432 | tf_op jit(solution)/shard_map/dot_general | solution.py:39
  347.3 9.5 %fusion.5 = f32[1728,1152]{1,0:T(8,128)} fusion(f32[1728,1152]{1,0:T(8,128)S(1)} %bitcast.86, f16[864,1152]{1,0:T(8,128)(2,1)} %get-tuple-element.38, f16[864,1152]{1,0:T(8,128)(2,1)} %get-tuple-element.37, f16[864,1152]{1,0:T(8,128)(2,1)} %copy-done.13, f16[864,1152]{1,0:T(8,128)(2,1)} %copy-done.12, bf16[256,5184]{0,1:T(8,128)(2,1)} %copy-done.24, ...), kind=kOutput, calls=%fused_computation.13 | convolution fusion | flops 1042292736 | bytes 25362432 | tf_op jit(solution)/shard_map/dot_general | solution.py:39
  356.9 4.5 %broadcast_select_fusion.1 = (f16[864,1152]{1,0:T(8,128)(2,1)S(1)}, f16[864,1152]{1,0:T(8,128)(2,1)}) fusion(f16[864,1152]{1,0:T(8,128)(2,1)} %collective-permute-done.23, f16[864,1152]{1,0:T(8,128)(2,1)} %collective-permute-done.24, pred[]{:T(512)S(6)} %eq.2), kind=kLoop, calls=%fused_computation.69 | loop fusion | flops 1990656 | bytes 7962625 | tf_op jit(solution)/shard_map/jit(_where)/select_n | solution.py:53
  361.5 8.8 %fusion.3 = f32[1728,1152]{1,0:T(8,128)} fusion(f32[1728,1152]{1,0:T(8,128)S(1)} %bitcast.84, f16[864,1152]{1,0:T(8,128)(2,1)} %get-tuple-element.30, f16[864,1152]{1,0:T(8,128)(2,1)S(1)} %get-tuple-element.29, f16[864,1152]{1,0:T(8,128)(2,1)S(1)} %copy-done.11, f16[864,1152]{1,0:T(8,128)(2,1)S(1)} %copy-done.9, bf16[256,5184]{0,1:T(8,128)(2,1)} %copy-done.24, ...), kind=kOutput, calls=%fused_computation.7 | convolution fusion | flops 1042292736 | bytes 25362432 | tf_op jit(solution)/shard_map/dot_general | solution.py:39
  370.4 5.4 %fusion.7 = f32[1,1728,1152]{2,1,0:T(8,128)} fusion(f32[1728,1152]{1,0:T(8,128)S(1)} %bitcast.94, bf16[256,5184]{0,1:T(8,128)(2,1)S(1)} %copy-done.3, bf16[128,1152]{1,0:T(8,128)(2,1)S(1)} %copy-done.23, bf16[128,1152]{1,0:T(8,128)(2,1)S(1)} %copy-done.22), kind=kOutput, calls=%fused_computation.16 | convolution fusion | flops 1024376832 | bytes 17399808 | tf_op jit(solution)/shard_map/dot_general | solution.py:39
  375.9 4.7 %fusion.6 = f32[1,1728,1152]{2,1,0:T(8,128)} fusion(f32[1728,1152]{1,0:T(8,128)S(1)} %copy-done.7, bf16[256,5184]{0,1:T(8,128)(2,1)S(1)} %copy-done.3, bf16[128,1152]{1,0:T(8,128)(2,1)S(1)} %copy-done.23, bf16[128,1152]{1,0:T(8,128)(2,1)S(1)} %copy-done.22), kind=kOutput, calls=%fused_computation.15 | convolution fusion | flops 1024376832 | bytes 17399808 | tf_op jit(solution)/shard_map/dot_general | solution.py:39
  380.6 5.7 %fusion.8 = f32[1,1728,1152]{2,1,0:T(8,128)} fusion(f32[1728,1152]{1,0:T(8,128)S(1)} %bitcast.96, bf16[256,5184]{0,1:T(8,128)(2,1)S(1)} %copy-done.3, bf16[128,1152]{1,0:T(8,128)(2,1)S(1)} %collective-permute-done.28, bf16[128,1152]{1,0:T(8,128)(2,1)} %fusion.89), kind=kOutput, calls=%fused_computation.17 | convolution fusion | flops 1024376832 | bytes 17399808 | tf_op jit(solution)/shard_map/dot_general | solution.py:39
  (197 shorter events, 74.1 us)
Async XLA Ops:
  7.2 110.5 %all-reduce.3.cloned.1.call-start = ((), (), s32[]{:S(2)}) async-start(), calls=%async_computation | async-start | bytes 1179648 | tf_op jit(solution)/shard_map/psum | solution.py:67
  23.0 37.0 %collective-permute-start.2 = (f16[864,1152]{1,0:T(8,128)(2,1)}, f16[864,1152]{1,0:T(8,128)(2,1)}, u32[]{:S(2)}, u32[]{:S(2)}) collective-permute-start(f16[864,1152]{1,0:T(8,128)(2,1)} %fusion.54), channel_id=1, source_target_pairs={{0,4},{4,0},{8,12},{12,8},{16,20},{20,16},{24,28},{28,24},{1,5},{5... | collective-permute-start | bytes 5971976 | tf_op jit(solution)/shard_map/ppermute | solution.py:12
  23.0 25.6 %collective-permute-start.4 = (bf16[4,32,1152]{2,1,0:T(8,128)(2,1)}, bf16[4,32,1152]{2,1,0:T(8,128)(2,1)S(1)}, u32[]{:S(2)}, u32[]{:S(2)}) collective-permute-start(bf16[4,32,1152]{2,1,0:T(8,128)(2,1)} %get-tuple-element.47), channel_id=1, source_target_pairs={{0,2},{1,3},{2,0},{3,1},{4,6},{5,7},{6,4},{7,5},{8,10},{9,11},{10,... | collective-permute-start | bytes 884744 | tf_op jit(solution)/shard_map/ppermute | solution.py:21
  23.0 26.3 %collective-permute-start.5 = (bf16[4,32,1152]{2,1,0:T(8,128)(2,1)}, bf16[4,32,1152]{2,1,0:T(8,128)(2,1)S(1)}, u32[]{:S(2)}, u32[]{:S(2)}) collective-permute-start(bf16[4,32,1152]{2,1,0:T(8,128)(2,1)} %get-tuple-element.47), channel_id=1, source_target_pairs={{0,1},{1,2},{2,3},{3,0},{4,5},{5,6},{6,7},{7,4},{8,9},{9,10},{10,1... | collective-permute-start | bytes 884744 | tf_op jit(solution)/shard_map/ppermute | solution.py:21
  30.8 34.1 %collective-permute-start.1 = (f16[864,1152]{1,0:T(8,128)(2,1)}, f16[864,1152]{1,0:T(8,128)(2,1)S(1)}, u32[]{:S(2)}, u32[]{:S(2)}) collective-permute-start(f16[864,1152]{1,0:T(8,128)(2,1)} %get-tuple-element.16), channel_id=1, source_target_pairs={{0,4},{4,0},{8,12},{12,8},{16,20},{20,16},{24,28},{28,24},{1,5},{5... | collective-permute-start | bytes 5971976 | tf_op jit(solution)/shard_map/ppermute | solution.py:12
  31.5 37.9 %collective-permute-start = (f16[864,1152]{1,0:T(8,128)(2,1)S(1)}, f16[864,1152]{1,0:T(8,128)(2,1)S(1)}, u32[]{:S(2)}, u32[]{:S(2)}) collective-permute-start(f16[864,1152]{1,0:T(8,128)(2,1)S(1)} %get-tuple-element.15), channel_id=1, source_target_pairs={{0,4},{4,0},{8,12},{12,8},{16,20},{20,16},{24,28},{28,24},{1,5},{5... | collective-permute-start | bytes 5971976 | tf_op jit(solution)/shard_map/ppermute | solution.py:12
  48.6 30.0 %collective-permute-start.14 = (bf16[2,32,1152]{2,1,0:T(8,128)(2,1)}, bf16[2,32,1152]{2,1,0:T(8,128)(2,1)S(1)}, u32[]{:S(2)}, u32[]{:S(2)}) collective-permute-start(bf16[2,32,1152]{2,1,0:T(8,128)(2,1)} %collective-permute-done.13), channel_id=1, source_target_pairs={{0,3},{1,0},{2,1},{3,2},{4,7},{5,4},{6,5},{7,6},{8,11},{9,8},{10,9... | collective-permute-start | bytes 442376 | tf_op jit(solution)/shard_map/ppermute | solution.py:21
  49.3 30.0 %collective-permute-start.15 = (bf16[2,32,1152]{2,1,0:T(8,128)(2,1)}, bf16[2,32,1152]{2,1,0:T(8,128)(2,1)S(1)}, u32[]{:S(2)}, u32[]{:S(2)}) collective-permute-start(bf16[2,32,1152]{2,1,0:T(8,128)(2,1)} %collective-permute-done.13), channel_id=1, source_target_pairs={{0,2},{1,3},{2,0},{3,1},{4,6},{5,7},{6,4},{7,5},{8,10},{9,11},{10,... | collective-permute-start | bytes 442376 | tf_op jit(solution)/shard_map/ppermute | solution.py:21
  60.0 65.1 %collective-permute-start.16 = (bf16[2,32,1152]{2,1,0:T(8,128)(2,1)}, bf16[2,32,1152]{2,1,0:T(8,128)(2,1)}, u32[]{:S(2)}, u32[]{:S(2)}) collective-permute-start(bf16[2,32,1152]{2,1,0:T(8,128)(2,1)} %collective-permute-done.13), channel_id=1, source_target_pairs={{0,1},{1,2},{2,3},{3,0},{4,5},{5,6},{6,7},{7,4},{8,9},{9,10},{10,1... | collective-permute-start | bytes 442376 | tf_op jit(solution)/shard_map/ppermute | solution.py:21
  76.8 128.1 %all-reduce.5.cloned.1.call-start = ((), (), s32[]{:S(2)}) async-start(), calls=%async_computation.1 | async-start | bytes 1179648 | tf_op jit(solution)/shard_map/psum | solution.py:67
  128.9 17.2 %collective-permute-start.18 = (f16[864,1152]{1,0:T(8,128)(2,1)}, f16[864,1152]{1,0:T(8,128)(2,1)}, u32[]{:S(2)}, u32[]{:S(2)}) collective-permute-start(f16[864,1152]{1,0:T(8,128)(2,1)} %fusion.27), channel_id=1, source_target_pairs={{0,4},{4,0},{8,12},{12,8},{16,20},{20,16},{24,28},{28,24},{1,5},{5... | collective-permute-start | bytes 5971976 | tf_op jit(solution)/shard_map/ppermute | solution.py:12
  129.4 75.0 %collective-permute-start.19 = (f16[864,1152]{1,0:T(8,128)(2,1)}, f16[864,1152]{1,0:T(8,128)(2,1)}, u32[]{:S(2)}, u32[]{:S(2)}) collective-permute-start(f16[864,1152]{1,0:T(8,128)(2,1)} %fusion.27), channel_id=1, source_target_pairs={{0,8},{4,12},{8,0},{12,4},{16,24},{20,28},{24,16},{28,20},{1,9},{5... | collective-permute-start | bytes 5971976 | tf_op jit(solution)/shard_map/ppermute | solution.py:12
  131.7 17.7 %collective-permute-start.21 = (f16[864,1152]{1,0:T(8,128)(2,1)S(1)}, f16[864,1152]{1,0:T(8,128)(2,1)}, u32[]{:S(2)}, u32[]{:S(2)}) collective-permute-start(f16[864,1152]{1,0:T(8,128)(2,1)S(1)} %copy-done.14), channel_id=1, source_target_pairs={{0,4},{4,0},{8,12},{12,8},{16,20},{20,16},{24,28},{28,24},{1,5},{5... | collective-permute-start | bytes 5971976 | tf_op jit(solution)/shard_map/ppermute | solution.py:12
  139.2 65.2 %collective-permute-start.11 = (bf16[128,5184]{0,1:T(8,128)(2,1)}, bf16[128,5184]{0,1:T(8,128)(2,1)}, u32[]{:S(2)}, u32[]{:S(2)}) collective-permute-start(bf16[128,5184]{0,1:T(8,128)(2,1)} %pad_maximum_fusion.7), channel_id=1, source_target_pairs={{0,8},{4,12},{8,0},{12,4},{16,24},{20,28},{24,16},{28,20},{1,9},{5... | collective-permute-start | bytes 3981320 | tf_op jit(solution)/shard_map/ppermute | solution.py:12
  164.9 158.6 %collective-permute-start.23 = (f16[864,1152]{1,0:T(8,128)(2,1)}, f16[864,1152]{1,0:T(8,128)(2,1)}, u32[]{:S(2)}, u32[]{:S(2)}) collective-permute-start(f16[864,1152]{1,0:T(8,128)(2,1)} %fusion.25), channel_id=1, source_target_pairs={{0,8},{4,12},{8,0},{12,4},{16,24},{20,28},{24,16},{28,20},{1,9},{5... | collective-permute-start | bytes 5971976 | tf_op jit(solution)/shard_map/ppermute | solution.py:12
  165.5 124.2 %collective-permute-start.9 = (f16[864,1152]{1,0:T(8,128)(2,1)}, f16[864,1152]{1,0:T(8,128)(2,1)}, u32[]{:S(2)}, u32[]{:S(2)}) collective-permute-start(f16[864,1152]{1,0:T(8,128)(2,1)} %fusion.29), channel_id=1, source_target_pairs={{0,8},{4,12},{8,0},{12,4},{16,24},{20,28},{24,16},{28,20},{1,9},{5... | collective-permute-start | bytes 5971976 | tf_op jit(solution)/shard_map/ppermute | solution.py:12
  204.4 86.8 %collective-permute-start.12 = (bf16[128,5184]{0,1:T(8,128)(2,1)}, bf16[128,5184]{0,1:T(8,128)(2,1)}, u32[]{:S(2)}, u32[]{:S(2)}) collective-permute-start(bf16[128,5184]{0,1:T(8,128)(2,1)} %collective-permute-done.11), channel_id=1, source_target_pairs={{0,4},{4,0},{8,12},{12,8},{16,20},{20,16},{24,28},{28,24},{1,5},{5... | collective-permute-start | bytes 3981320 | tf_op jit(solution)/shard_map/ppermute | solution.py:12
  204.4 121.6 %collective-permute-start.20 = (f16[864,1152]{1,0:T(8,128)(2,1)}, f16[864,1152]{1,0:T(8,128)(2,1)}, u32[]{:S(2)}, u32[]{:S(2)}) collective-permute-start(f16[864,1152]{1,0:T(8,128)(2,1)} %collective-permute-done.19), channel_id=1, source_target_pairs={{0,4},{4,0},{8,12},{12,8},{16,20},{20,16},{24,28},{28,24},{1,5},{5... | collective-permute-start | bytes 5971976 | tf_op jit(solution)/shard_map/ppermute | solution.py:12
  213.3 110.7 %collective-permute-start.27 = (bf16[128,5184]{0,1:T(8,128)(2,1)S(1)}, bf16[128,5184]{0,1:T(8,128)(2,1)S(1)}, u32[]{:S(2)}, u32[]{:S(2)}) collective-permute-start(bf16[128,5184]{0,1:T(8,128)(2,1)S(1)} %pad_maximum_fusion.8), channel_id=1, source_target_pairs={{0,8},{4,12},{8,0},{12,4},{16,24},{20,28},{24,16},{28,20},{1,9},{5... | collective-permute-start | bytes 3981320 | tf_op jit(solution)/shard_map/ppermute | solution.py:12
  289.7 33.8 %collective-permute-start.25 = (bf16[128,1152]{1,0:T(8,128)(2,1)S(1)}, bf16[128,1152]{1,0:T(8,128)(2,1)}, u32[]{:S(2)}, u32[]{:S(2)}) collective-permute-start(bf16[128,1152]{1,0:T(8,128)(2,1)S(1)} %fusion.90), channel_id=1, source_target_pairs={{0,8},{4,12},{8,0},{12,4},{16,24},{20,28},{24,16},{28,20},{1,9},{5... | collective-permute-start | bytes 884744 | tf_op jit(solution)/shard_map/ppermute | solution.py:12
  291.2 41.4 %collective-permute-start.10 = (f16[864,1152]{1,0:T(8,128)(2,1)}, f16[864,1152]{1,0:T(8,128)(2,1)S(1)}, u32[]{:S(2)}, u32[]{:S(2)}) collective-permute-start(f16[864,1152]{1,0:T(8,128)(2,1)} %collective-permute-done.9), channel_id=1, source_target_pairs={{0,4},{4,0},{8,12},{12,8},{16,20},{20,16},{24,28},{28,24},{1,5},{5... | collective-permute-start | bytes 5971976 | tf_op jit(solution)/shard_map/ppermute | solution.py:12
  323.5 37.8 %collective-permute-start.26 = (bf16[128,1152]{1,0:T(8,128)(2,1)}, bf16[128,1152]{1,0:T(8,128)(2,1)S(1)}, u32[]{:S(2)}, u32[]{:S(2)}) collective-permute-start(bf16[128,1152]{1,0:T(8,128)(2,1)} %collective-permute-done.25), channel_id=1, source_target_pairs={{0,4},{4,0},{8,12},{12,8},{16,20},{20,16},{24,28},{28,24},{1,5},{5... | collective-permute-start | bytes 884744 | tf_op jit(solution)/shard_map/ppermute | solution.py:12
  324.0 32.8 %collective-permute-start.24 = (f16[864,1152]{1,0:T(8,128)(2,1)}, f16[864,1152]{1,0:T(8,128)(2,1)}, u32[]{:S(2)}, u32[]{:S(2)}) collective-permute-start(f16[864,1152]{1,0:T(8,128)(2,1)} %collective-permute-done.23), channel_id=1, source_target_pairs={{0,4},{4,0},{8,12},{12,8},{16,20},{20,16},{24,28},{28,24},{1,5},{5... | collective-permute-start | bytes 5971976 | tf_op jit(solution)/shard_map/ppermute | solution.py:12
  326.0 54.6 %collective-permute-start.28 = (bf16[128,1152]{1,0:T(8,128)(2,1)}, bf16[128,1152]{1,0:T(8,128)(2,1)S(1)}, u32[]{:S(2)}, u32[]{:S(2)}) collective-permute-start(bf16[128,1152]{1,0:T(8,128)(2,1)} %fusion.89), channel_id=1, source_target_pairs={{0,8},{4,12},{8,0},{12,4},{16,24},{20,28},{24,16},{28,20},{1,9},{5... | collective-permute-start | bytes 884744 | tf_op jit(solution)/shard_map/ppermute | solution.py:12
  (53 other events, 555.5 us)
Sparse Core Ops, SparseCore 0:
  76.9 40.7 all-reduce.2
  159.9 37.8 all-reduce.4
